TPU v7x, 512 devices: a whole 4x8x8 slice. The times are simulated.
512 devices in a mesh: tm: 128 (over z, y, core), swath: 4 (over x).
Axes of the slice: x: 4, y: 8, z: 8, core: 2. Of those that a mesh axis runs over, the one named last changes fastest.
Arguments:
- design: bfloat16 [128, 2048, 512], P('tm', 'swath'), may hold values from -6 to 6
- process: bfloat16 [128, 512, 512], P('tm', 'swath')
- prior_prec: float32 [128, 512], P('tm', 'swath'), may hold values from 0.05 to 0.5
- routes: int32 [128, 16], P('tm', 'swath'), may hold values from -1 to 127, as said below
- counts: int32 [128, 4], P('tm', 'swath'), may hold values from 1 to 4
Outputs:
- reduced_diag: float32 [128, 512, 512], P('tm', 'swath')
- reduced_coupling: float32 [128, 512, 512], P('tm', 'swath')
Inputs may be any that keep to these rules, and one draw needn't show every extreme that they name: `routes`: each value is the holder's own time block i or i + 1, or -1 only where i + 1 would be 128; of one holder's 4 blocks, exactly 2 name i and the others i + 1 or -1.
All inputs are finite; a program needn't handle non-finite values.
Results may differ from a plain program's by a relative error of at most 0.00073.
Values may be sent and summed in bfloat16 or wider, within the bound.
No kernel may reach another device: no remote copies, remote signals or barrier semaphores. Data moves between devices by JAX's collectives and lax.ppermute only.
A program may use at most 64 MiB of HBM per device.

v0:
```python
import jax
import jax.numpy as jnp
from jax import lax
from jax.sharding import PartitionSpec as P

LEVELS = 3


def passed_along(block, axis, distance):
    devices = range(lax.axis_size(axis))
    route = [(i - distance, i) for i in devices if i - distance in devices]
    return lax.ppermute(block, axis, route)


def tri_solve(factor, right):
    return lax.linalg.triangular_solve(factor, right, left_side=True, lower=True)


def inner_rows(left_side, right_side):
    return lax.dot_general(
        left_side,
        right_side,
        (((0,), (0,)), ((), ())),
        precision=lax.Precision.HIGHEST,
        preferred_element_type=jnp.float32,
    )


def compact(scaled, wanted, slot_count):
    sort_key = jnp.where(wanted, 0, 1).astype(jnp.int32)
    picked = jnp.argsort(sort_key, stable=True)[:slot_count]
    kept = jnp.take(sort_key, picked) == 0
    return jnp.where(kept[:, None, None], scaled[picked], 0.0).astype(jnp.bfloat16)


def shards(design, process, prior_prec, routes, counts):
    row_count = process.shape[1]
    order_size = process.shape[2]
    time_count = lax.axis_size("tm")
    my_time = lax.axis_index("tm")
    swath_index = lax.axis_index("swath")
    block_count = routes.shape[1]
    slot_count = block_count // 2
    block_rows = design.shape[1] // block_count
    total_slots = 2 * slot_count * block_rows * lax.axis_size("swath")
    row_start = swath_index * row_count
    raw_rows = design[0].reshape(block_count, block_rows, order_size).astype(jnp.float32)
    mean_sq = jnp.mean(raw_rows * raw_rows, axis=-1, keepdims=True)
    scaled = raw_rows * lax.rsqrt(4.0 * total_slots * (mean_sq + 1e-06))
    live = jnp.arange(block_count) < counts[0, 0]
    target = routes[0]
    own_blocks = compact(scaled, live & (target == my_time), slot_count)
    ahead_blocks = compact(scaled, live & (target == my_time + 1), slot_count)
    incoming, previous = passed_along((ahead_blocks, process), "tm", 1)
    gram_input = jnp.concatenate([own_blocks, incoming], axis=0).reshape(-1, order_size)
    shard_rows = lax.all_gather(gram_input, "swath", axis=0, tiled=True)
    columns = lax.dynamic_slice_in_dim(shard_rows, row_start, row_count, 1)
    gram = lax.dot_general(
        columns, shard_rows, (((0,), (0,)), ((), ())), preferred_element_type=jnp.float32
    )
    unit_rows = jnp.arange(order_size)[None, :] == jnp.arange(row_count)[:, None] + row_start
    diag_rows = previous[0].astype(jnp.float32) + process[0].astype(jnp.float32) + gram
    diag_rows = diag_rows + jnp.where(unit_rows, prior_prec[0][:, None], 0.0)
    coup_rows = -process[0].astype(jnp.float32)
    unit_full = jnp.eye(order_size, dtype=jnp.float32)
    for level in range(LEVELS):
        distance = 2**level
        full_diag, full_coup = (
            lax.all_gather(diag_rows, "swath", axis=0, tiled=True),
            lax.all_gather(coup_rows, "swath", axis=0, tiled=True),
        )
        factor = jnp.linalg.cholesky(full_diag)
        solved = tri_solve(factor, full_coup)
        own_cols = lax.dynamic_slice_in_dim(solved, row_start, row_count, 1)
        eliminated = inner_rows(own_cols, solved)
        left_term = passed_along(eliminated, "tm", distance)
        far_factor, far_solved = passed_along((factor, solved), "tm", -distance)
        has_partner = my_time + distance < time_count
        far_factor = jnp.where(has_partner, far_factor, unit_full)
        cross = tri_solve(far_factor, full_coup.T)
        cross_cols = lax.dynamic_slice_in_dim(cross, row_start, row_count, 1)
        right_term = inner_rows(cross_cols, cross)
        new_coupling = inner_rows(cross_cols, far_solved)
        diag_rows = diag_rows - left_term - jnp.where(has_partner, right_term, 0.0)
        coup_rows = -new_coupling
    return (diag_rows[None], coup_rows[None])


def solution(mesh):
    return jax.shard_map(
        shards,
        mesh=mesh,
        in_specs=(
            P("tm", "swath", None),
            P("tm", "swath", None),
            P("tm", "swath"),
            P("tm", "swath"),
            P("tm", "swath"),
        ),
        out_specs=(P("tm", "swath", None), P("tm", "swath", None)),
        check_vma=False,
    )
```

profile of v0, /device:TPU:16, one launch (start us, length us, event | category | flops | bytes accessed | tf_op | source)
XLA Modules:
  0.0 882.1 jit_solution(11233047935860242572)
XLA Ops:
  28.9 35.5 %all-gather.9.cloned.1.call-done = bf16[2048,512]{1,0:T(8,128)(2,1)} async-done(((bf16[512,512]{1,0:T(8,128)(2,1)}), bf16[2048,512]{1,0:T(8,128)(2,1)}) %all-gather.9.cloned.1.call-update) | async-done | bytes 2097168 | tf_op jit(solution)/shard_map/all_gather | solution.py:56
  68.6 30.6 %all-gather.11.cloned.1.call-done = f32[512,512]{0,1:T(8,128)} async-done(((f32[128,512]{0,1:T(8,128)}), f32[512,512]{0,1:T(8,128)}) %all-gather.11.cloned.1.call-update) | async-done | bytes 1048592 | tf_op jit(solution)/shard_map/all_gather | solution.py:69
  101.1 11.7 %cholesky.374 = f32[128,128]{1,0:T(8,128)S(1)} custom-call(f32[128,128]{1,0:T(8,128)S(1)} %cholesky.586), custom_call_target="Cholesky" | custom-call | tf_op jit(solution)/shard_map/jit(cholesky)/cholesky | solution.py:72
  123.5 11.7 %cholesky.393 = f32[128,128]{1,0:T(8,128)S(1)} custom-call(f32[128,128]{1,0:T(8,128)S(1)} %cholesky.590), custom_call_target="Cholesky" | custom-call | tf_op jit(solution)/shard_map/jit(cholesky)/cholesky | solution.py:72
  146.1 11.7 %cholesky.414 = f32[128,128]{1,0:T(8,128)S(1)} custom-call(f32[128,128]{1,0:T(8,128)S(1)} %cholesky.595), custom_call_target="Cholesky" | custom-call | tf_op jit(solution)/shard_map/jit(cholesky)/cholesky | solution.py:72
  168.3 11.7 %cholesky.431 = f32[128,128]{1,0:T(8,128)S(1)} custom-call(f32[128,128]{1,0:T(8,128)S(1)} %convolution_subtract_fusion.14), custom_call_target="Cholesky" | custom-call | tf_op jit(solution)/shard_map/jit(cholesky)/cholesky | solution.py:72
  193.0 39.3 %custom-call.37 = f32[4,128,128]{1,2,0:T(8,128)S(1)} custom-call(f32[4,128,128]{2,1,0:T(8,128)S(1)} %get-tuple-element.47), custom_call_target="InvertDiagBlocksLowerTriangular" | custom-call | tf_op jit(solution)/shard_map/triangular_solve/custom-call.3 | solution.py:16
  262.2 40.7 %custom-call.38 = f32[4,128,128]{1,2,0:T(8,128)} custom-call(f32[4,128,128]{2,1,0:T(8,128)} %get-tuple-element.48), custom_call_target="InvertDiagBlocksLowerTriangular" | custom-call | tf_op jit(solution)/shard_map/triangular_solve/custom-call.3 | solution.py:16
  314.4 12.3 %collective-permute-done.4 = f32[512,512]{1,0:T(8,128)S(1)} collective-permute-done((f32[512,512]{1,0:T(8,128)S(1)}, f32[512,512]{1,0:T(8,128)S(1)}, u32[]{:S(2)}, u32[]{:S(2)}) %collective-permute-start.4) | collective-permute-done | bytes 1048608 | tf_op jit(solution)/shard_map/ppermute | solution.py:12
  328.6 15.1 %all-gather.13.cloned.1.call-done = f32[512,512]{0,1:T(8,128)} async-done(((f32[128,512]{0,1:T(8,128)}), f32[512,512]{0,1:T(8,128)}) %all-gather.13.cloned.1.call-update) | async-done | bytes 1048592 | tf_op jit(solution)/shard_map/all_gather | solution.py:69
  345.6 11.7 %cholesky.446 = f32[128,128]{1,0:T(8,128)S(1)} custom-call(f32[128,128]{1,0:T(8,128)S(1)} %cholesky.599), custom_call_target="Cholesky" | custom-call | tf_op jit(solution)/shard_map/jit(cholesky)/cholesky | solution.py:72
  368.0 11.7 %cholesky.465 = f32[128,128]{1,0:T(8,128)S(1)} custom-call(f32[128,128]{1,0:T(8,128)S(1)} %cholesky.603), custom_call_target="Cholesky" | custom-call | tf_op jit(solution)/shard_map/jit(cholesky)/cholesky | solution.py:72
  390.4 11.7 %cholesky.486 = f32[128,128]{1,0:T(8,128)S(1)} custom-call(f32[128,128]{1,0:T(8,128)S(1)} %cholesky.608), custom_call_target="Cholesky" | custom-call | tf_op jit(solution)/shard_map/jit(cholesky)/cholesky | solution.py:72
  412.5 11.7 %cholesky.503 = f32[128,128]{1,0:T(8,128)S(1)} custom-call(f32[128,128]{1,0:T(8,128)S(1)} %convolution_subtract_fusion.13), custom_call_target="Cholesky" | custom-call | tf_op jit(solution)/shard_map/jit(cholesky)/cholesky | solution.py:72
  437.3 39.3 %custom-call.42 = f32[4,128,128]{1,2,0:T(8,128)S(1)} custom-call(f32[4,128,128]{2,1,0:T(8,128)S(1)} %get-tuple-element.49), custom_call_target="InvertDiagBlocksLowerTriangular" | custom-call | tf_op jit(solution)/shard_map/triangular_solve/custom-call.3 | solution.py:16
  490.7 15.6 %collective-permute-done.6 = f32[512,512]{1,0:T(8,128)S(1)} collective-permute-done((f32[512,512]{1,0:T(8,128)S(1)}, f32[512,512]{1,0:T(8,128)S(1)}, u32[]{:S(2)}, u32[]{:S(2)}) %collective-permute-start.6) | collective-permute-done | bytes 1048608 | tf_op jit(solution)/shard_map/ppermute | solution.py:12
  517.3 40.7 %custom-call.43 = f32[4,128,128]{1,2,0:T(8,128)} custom-call(f32[4,128,128]{2,1,0:T(8,128)} %get-tuple-element.50), custom_call_target="InvertDiagBlocksLowerTriangular" | custom-call | tf_op jit(solution)/shard_map/triangular_solve/custom-call.3 | solution.py:16
  570.0 23.3 %collective-permute-done.7 = f32[512,512]{1,0:T(8,128)S(1)} collective-permute-done((f32[512,512]{1,0:T(8,128)S(1)}, f32[512,512]{1,0:T(8,128)S(1)}, u32[]{:S(2)}, u32[]{:S(2)}) %collective-permute-start.7) | collective-permute-done | bytes 1048608 | tf_op jit(solution)/shard_map/ppermute | solution.py:12
  601.6 11.7 %cholesky.518 = f32[128,128]{1,0:T(8,128)S(1)} custom-call(f32[128,128]{1,0:T(8,128)S(1)} %cholesky.612), custom_call_target="Cholesky" | custom-call | tf_op jit(solution)/shard_map/jit(cholesky)/cholesky | solution.py:72
  624.0 11.7 %cholesky.537 = f32[128,128]{1,0:T(8,128)S(1)} custom-call(f32[128,128]{1,0:T(8,128)S(1)} %cholesky.616), custom_call_target="Cholesky" | custom-call | tf_op jit(solution)/shard_map/jit(cholesky)/cholesky | solution.py:72
  668.6 12.1 %cholesky.575 = f32[128,128]{1,0:T(8,128)S(1)} custom-call(f32[128,128]{1,0:T(8,128)S(1)} %convolution_subtract_fusion.12), custom_call_target="Cholesky" | custom-call | tf_op jit(solution)/shard_map/jit(cholesky)/cholesky | solution.py:72
  693.9 39.3 %custom-call.47 = f32[4,128,128]{1,2,0:T(8,128)S(1)} custom-call(f32[4,128,128]{2,1,0:T(8,128)S(1)} %get-tuple-element.51), custom_call_target="InvertDiagBlocksLowerTriangular" | custom-call | tf_op jit(solution)/shard_map/triangular_solve/custom-call.3 | solution.py:16
  751.6 59.3 %collective-permute-done.9 = f32[512,512]{1,0:T(8,128)S(1)} collective-permute-done((f32[512,512]{1,0:T(8,128)S(1)}, f32[512,512]{1,0:T(8,128)S(1)}, u32[]{:S(2)}, u32[]{:S(2)}) %collective-permute-start.9) | collective-permute-done | bytes 1048608 | tf_op jit(solution)/shard_map/ppermute | solution.py:12
  822.2 40.7 %custom-call.48 = f32[4,128,128]{1,2,0:T(8,128)} custom-call(f32[4,128,128]{2,1,0:T(8,128)} %get-tuple-element.52), custom_call_target="InvertDiagBlocksLowerTriangular" | custom-call | tf_op jit(solution)/shard_map/triangular_solve/custom-call.3 | solution.py:16
  (308 shorter events, 351.0 us)
Async XLA Ops:
  7.2 57.3 %all-gather.9.cloned.1.call-start = ((), (), s32[]{:S(2)}) async-start(), calls=%async_computation | async-start | bytes 2621440 | tf_op jit(solution)/shard_map/all_gather | solution.py:56
  13.1 9.3 %copy-start.12 = (bf16[1,128,512]{2,1,0:T(8,128)(2,1)S(1)}, bf16[1,128,512]{2,1,0:T(8,128)(2,1)}, u32[]{:S(2)}) copy-start(bf16[1,128,512]{2,1,0:T(8,128)(2,1)} %param.11) | copy-start | bytes 393220
  13.7 50.7 %copy-start.13 = (f32[1,128]{1,0:T(1,128)S(1)}, f32[1,128]{1,0:T(1,128)}, u32[]{:S(2)}) copy-start(f32[1,128]{1,0:T(1,128)} %param.12) | copy-start | bytes 1540
  13.9 7.7 collective-permute-start.1
  22.4 76.8 %all-gather.11.cloned.1.call-start = ((), (), s32[]{:S(2)}) async-start(), calls=%async_computation.1 | async-start | bytes 1310720 | tf_op jit(solution)/shard_map/all_gather | solution.py:69
  22.6 6.3 collective-permute-start
  67.8 164.6 %all-gather.21.cloned.1.call-start = ((), (), s32[]{:S(2)}) async-start(), calls=%async_computation.6 | async-start | bytes 1310720 | tf_op jit(solution)/shard_map/all_gather | solution.py:70
  68.6 275.1 %all-gather.13.cloned.1.call-start = ((), (), s32[]{:S(2)}) async-start(), calls=%async_computation.2 | async-start | bytes 1310720 | tf_op jit(solution)/shard_map/all_gather | solution.py:69
  236.9 14.2 %collective-permute-start.3 = (f32[512,512]{1,0:T(8,128)S(1)}, f32[512,512]{1,0:T(8,128)S(1)}, u32[]{:S(2)}, u32[]{:S(2)}) collective-permute-start(f32[512,512]{1,0:T(8,128)S(1)} %get-tuple-element.110), channel_id=1, source_target_pairs={{4,0},{8,4},{12,8},{16,12},{20,16},{24,20},{28,24},{32,28},{36,32}... | collective-permute-start | bytes 3145736 | tf_op jit(solution)/shard_map/ppermute | solution.py:12
  243.7 64.2 %collective-permute-start.2 = (f32[128,512]{0,1:T(8,128)}, f32[128,512]{0,1:T(8,128)S(1)}, u32[]{:S(2)}, u32[]{:S(2)}) collective-permute-start(f32[128,512]{0,1:T(8,128)} %fusion.103), channel_id=1, source_target_pairs={{0,4},{4,8},{8,12},{12,16},{16,20},{20,24},{24,28},{28,32},{32,36}... | collective-permute-start | bytes 786440 | tf_op jit(solution)/shard_map/ppermute | solution.py:12
  310.5 166.1 %all-gather.15.cloned.1.call-start = ((), (), s32[]{:S(2)}) async-start(), calls=%async_computation.3 | async-start | bytes 1310720 | tf_op jit(solution)/shard_map/all_gather | solution.py:70
  310.6 16.1 %collective-permute-start.4 = (f32[512,512]{1,0:T(8,128)S(1)}, f32[512,512]{1,0:T(8,128)S(1)}, u32[]{:S(2)}, u32[]{:S(2)}) collective-permute-start(f32[512,512]{1,0:T(8,128)S(1)} %pad_maximum_fusion), channel_id=1, source_target_pairs={{4,0},{8,4},{12,8},{16,12},{20,16},{24,20},{28,24},{32,28},{36,32}... | collective-permute-start | bytes 3145736 | tf_op jit(solution)/shard_map/ppermute | solution.py:12
  328.2 271.6 %all-gather.17.cloned.1.call-start = ((), (), s32[]{:S(2)}) async-start(), calls=%async_computation.4 | async-start | bytes 1310720 | tf_op jit(solution)/shard_map/all_gather | solution.py:69
  476.6 6.1 copy-start.1
  480.3 25.9 %collective-permute-start.6 = (f32[512,512]{1,0:T(8,128)S(1)}, f32[512,512]{1,0:T(8,128)S(1)}, u32[]{:S(2)}, u32[]{:S(2)}) collective-permute-start(f32[512,512]{1,0:T(8,128)S(1)} %get-tuple-element.108), channel_id=1, source_target_pairs={{8,0},{12,4},{16,8},{20,12},{24,16},{28,20},{32,24},{36,28},{40,32... | collective-permute-start | bytes 3145736 | tf_op jit(solution)/shard_map/ppermute | solution.py:12
  486.9 77.9 %collective-permute-start.5 = (f32[128,512]{0,1:T(8,128)}, f32[128,512]{0,1:T(8,128)S(1)}, u32[]{:S(2)}, u32[]{:S(2)}) collective-permute-start(f32[128,512]{0,1:T(8,128)} %fusion.101), channel_id=1, source_target_pairs={{0,8},{4,12},{8,16},{12,20},{16,24},{20,28},{24,32},{28,36},{32,40... | collective-permute-start | bytes 786440 | tf_op jit(solution)/shard_map/ppermute | solution.py:12
  558.1 4.2 copy-start.10
  567.3 165.9 %all-gather.19.cloned.1.call-start = ((), (), s32[]{:S(2)}) async-start(), calls=%async_computation.5 | async-start | bytes 1310720 | tf_op jit(solution)/shard_map/all_gather | solution.py:70
  567.4 26.0 %collective-permute-start.7 = (f32[512,512]{1,0:T(8,128)S(1)}, f32[512,512]{1,0:T(8,128)S(1)}, u32[]{:S(2)}, u32[]{:S(2)}) collective-permute-start(f32[512,512]{1,0:T(8,128)S(1)} %pad_maximum_fusion.2), channel_id=1, source_target_pairs={{8,0},{12,4},{16,8},{20,12},{24,16},{28,20},{32,24},{36,28},{40,32... | collective-permute-start | bytes 3145736 | tf_op jit(solution)/shard_map/ppermute | solution.py:12
  733.2 6.1 copy-start
  736.9 74.0 %collective-permute-start.9 = (f32[512,512]{1,0:T(8,128)S(1)}, f32[512,512]{1,0:T(8,128)S(1)}, u32[]{:S(2)}, u32[]{:S(2)}) collective-permute-start(f32[512,512]{1,0:T(8,128)S(1)} %get-tuple-element.106), channel_id=1, source_target_pairs={{16,0},{20,4},{24,8},{28,12},{32,16},{36,20},{40,24},{44,28},{48,3... | collective-permute-start | bytes 3145736 | tf_op jit(solution)/shard_map/ppermute | solution.py:12
  740.9 131.4 %collective-permute-start.10 = (f32[512,512]{1,0:T(8,128)S(1)}, f32[512,512]{1,0:T(8,128)}, u32[]{:S(2)}, u32[]{:S(2)}) collective-permute-start(f32[512,512]{1,0:T(8,128)S(1)} %pad_maximum_fusion.4), channel_id=1, source_target_pairs={{16,0},{20,4},{24,8},{28,12},{32,16},{36,20},{40,24},{44,28},{48,3... | collective-permute-start | bytes 3145736 | tf_op jit(solution)/shard_map/ppermute | solution.py:12
  745.4 124.3 %collective-permute-start.8 = (f32[128,512]{0,1:T(8,128)}, f32[128,512]{0,1:T(8,128)S(1)}, u32[]{:S(2)}, u32[]{:S(2)}) collective-permute-start(f32[128,512]{0,1:T(8,128)} %fusion.99), channel_id=1, source_target_pairs={{0,16},{4,20},{8,24},{12,28},{16,32},{20,36},{24,40},{28,44},{32,4... | collective-permute-start | bytes 786440 | tf_op jit(solution)/shard_map/ppermute | solution.py:12
  862.9 4.2 copy-start.11
  (8 other events, 17.1 us)
Sparse Core Ops, SparseCore 0:
  22.5 41.8 all-gather.8
  67.9 31.2 all-gather.10
  101.9 32.4 all-gather.20
  310.6 33.0 all-gather.12
  346.2 30.5 all-gather.14
  567.5 32.2 all-gather.16
  602.4 30.6 all-gather.18
where the time goes:
time: 894 us; the launch traced here: 882 us
  other arithmetic  487 us (54%)
  waiting for transfers between devices  210 us (23%)
  local copies, waits for them, and re-layouts  64.4 us (7%)
  matrix products  64 us (7%)
  starting transfers between devices  32.1 us (4%)
  between operations  23.4 us (3%)
    another operation x19, other arithmetic, tri_solve(): lax.linalg.triangular_solve(factor, right, left_side=True, lower=True)  242 us
    another operation x45, other arithmetic, shards(): factor = jnp.linalg.cholesky(full_diag)  238 us
    ppermute x11, waiting for transfers between devices, passed_along(): return lax.ppermute(block, axis, route)  124 us
    another operation x79, local copies, waits for them, and re-layouts, tri_solve(): lax.linalg.triangular_solve(factor, right, left_side=True, lower=True)  55.7 us
    all_gather x3, waiting for transfers between devices, shards(): lax.all_gather(diag_rows, 'swath', axis=0, tiled=True)  50.5 us
    all_gather x1, waiting for transfers between devices, shards(): shard_rows = lax.all_gather(gram_input, 'swath', axis=0, tiled=True)  35.5 us
    another operation x42, matrix products, tri_solve(): lax.linalg.triangular_solve(factor, right, left_side=True, lower=True)  35 us
    ppermute x11, starting transfers between devices, passed_along(): return lax.ppermute(block, axis, route)  31.4 us
  transfers between devices with their start and end apart: 18, of which 11 were waited for; matrix products, arithmetic and copies ran while one was open for 66% of the time, Pallas kernels for 0%

commit v1 on v0

--- a/solution.py
+++ b/solution.py
@@ -53,7 +53,16 @@
     ahead_blocks = compact(scaled, live & (target == my_time + 1), slot_count)
     incoming, previous = passed_along((ahead_blocks, process), "tm", 1)
     gram_input = jnp.concatenate([own_blocks, incoming], axis=0).reshape(-1, order_size)
-    shard_rows = lax.all_gather(gram_input, "swath", axis=0, tiled=True)
+    ways = lax.axis_size("swath")
+    up = [(d, (d + 1) % ways) for d in range(ways)]
+    down = [(d, (d - 1) % ways) for d in range(ways)]
+    earlier, later = ([gram_input], [gram_input])
+    for _ in range(ways // 2):
+        earlier.append(lax.ppermute(earlier[-1], "swath", up))
+    for _ in range((ways - 1) // 2):
+        later.append(lax.ppermute(later[-1], "swath", down))
+    line = jnp.concatenate([*earlier[::-1], *later[1:]], axis=0)
+    shard_rows = jnp.roll(line, (lax.axis_index("swath") - ways // 2) * gram_input.shape[0], axis=0)
     columns = lax.dynamic_slice_in_dim(shard_rows, row_start, row_count, 1)
     gram = lax.dot_general(
         columns, shard_rows, (((0,), (0,)), ((), ())), preferred_element_type=jnp.float32

time: 894 us -> 826 us (0.924)
  the two profiles are of different devices: /device:TPU:16 before, /device:TPU:48 now
where the time goes in v1:
time: 826 us; the launch traced here: 820 us
  other arithmetic  496 us (60%)
  waiting for transfers between devices  114 us (14%)
  matrix products  75.9 us (9%)
  local copies, waits for them, and re-layouts  65.3 us (8%)
  starting transfers between devices  45.5 us (6%)
  between operations  23.6 us (3%)
    another operation x19, other arithmetic, tri_solve(): lax.linalg.triangular_solve(factor, right, left_side=True, lower=True)  248 us
    another operation x45, other arithmetic, shards(): factor = jnp.linalg.cholesky(full_diag)  238 us
    all_gather x3, waiting for transfers between devices, shards(): lax.all_gather(diag_rows, 'swath', axis=0, tiled=True)  56.6 us
    another operation x79, local copies, waits for them, and re-layouts, tri_solve(): lax.linalg.triangular_solve(factor, right, left_side=True, lower=True)  56.5 us
    another operation x42, matrix products, tri_solve(): lax.linalg.triangular_solve(factor, right, left_side=True, lower=True)  45.5 us
    ppermute x11, waiting for transfers between devices, passed_along(): return lax.ppermute(block, axis, route)  39.5 us
    ppermute x11, starting transfers between devices, passed_along(): return lax.ppermute(block, axis, route)  34.2 us
    dot_general x9, matrix products, inner_rows(): lax.dot_general(left_side, right_side, (((0,), (0,)), ((), ())), precisio...  22.9 us
  transfers between devices with their start and end apart: 20, of which 9 were waited for; matrix products, arithmetic and copies ran while one was open for 75% of the time, Pallas kernels for 0%

profile of v1, /device:TPU:48, one launch (start us, length us, event | category | flops | bytes accessed | tf_op | source)
XLA Modules:
  0.0 820.5 jit_solution(3685771204073556627)
XLA Ops:
  25.0 11.8 %collective-permute-done.2 = bf16[512,512]{1,0:T(8,128)(2,1)S(1)} collective-permute-done((bf16[512,512]{1,0:T(8,128)(2,1)S(1)}, bf16[512,512]{1,0:T(8,128)(2,1)S(1)}, u32[]{:S(2)}, u32[]{:S(2)}) %collective-permute-start.2) | collective-permute-done | bytes 524320 | tf_op jit(solution)/shard_map/ppermute | solution.py:61
  55.8 36.9 %all-gather.8.cloned.1.call-done = f32[512,512]{0,1:T(8,128)} async-done(((f32[128,512]{0,1:T(8,128)}), f32[512,512]{0,1:T(8,128)}) %all-gather.8.cloned.1.call-update) | async-done | bytes 1048592 | tf_op jit(solution)/shard_map/all_gather | solution.py:78
  95.8 11.7 %cholesky.374 = f32[128,128]{1,0:T(8,128)S(1)} custom-call(f32[128,128]{1,0:T(8,128)S(1)} %cholesky.586), custom_call_target="Cholesky" | custom-call | tf_op jit(solution)/shard_map/jit(cholesky)/cholesky | solution.py:81
  118.1 11.7 %cholesky.393 = f32[128,128]{1,0:T(8,128)S(1)} custom-call(f32[128,128]{1,0:T(8,128)S(1)} %cholesky.590), custom_call_target="Cholesky" | custom-call | tf_op jit(solution)/shard_map/jit(cholesky)/cholesky | solution.py:81
  141.8 11.7 %cholesky.414 = f32[128,128]{1,0:T(8,128)S(1)} custom-call(f32[128,128]{1,0:T(8,128)S(1)} %cholesky.595), custom_call_target="Cholesky" | custom-call | tf_op jit(solution)/shard_map/jit(cholesky)/cholesky | solution.py:81
  164.6 11.7 %cholesky.431 = f32[128,128]{1,0:T(8,128)S(1)} custom-call(f32[128,128]{1,0:T(8,128)S(1)} %convolution_subtract_fusion.14), custom_call_target="Cholesky" | custom-call | tf_op jit(solution)/shard_map/jit(cholesky)/cholesky | solution.py:81
  189.9 39.3 %custom-call.37 = f32[4,128,128]{1,2,0:T(8,128)S(1)} custom-call(f32[4,128,128]{2,1,0:T(8,128)S(1)} %get-tuple-element.47), custom_call_target="InvertDiagBlocksLowerTriangular" | custom-call | tf_op jit(solution)/shard_map/triangular_solve/custom-call.3 | solution.py:16
  255.5 40.8 %custom-call.38 = f32[4,128,128]{1,2,0:T(8,128)} custom-call(f32[4,128,128]{2,1,0:T(8,128)} %get-tuple-element.48), custom_call_target="InvertDiagBlocksLowerTriangular" | custom-call | tf_op jit(solution)/shard_map/triangular_solve/custom-call.3 | solution.py:16
  309.6 12.3 %collective-permute-done.7 = f32[512,512]{1,0:T(8,128)S(1)} collective-permute-done((f32[512,512]{1,0:T(8,128)S(1)}, f32[512,512]{1,0:T(8,128)S(1)}, u32[]{:S(2)}, u32[]{:S(2)}) %collective-permute-start.7) | collective-permute-done | bytes 1048608 | tf_op jit(solution)/shard_map/ppermute | solution.py:12
  323.6 15.2 %all-gather.10.cloned.1.call-done = f32[512,512]{0,1:T(8,128)} async-done(((f32[128,512]{0,1:T(8,128)}), f32[512,512]{0,1:T(8,128)}) %all-gather.10.cloned.1.call-update) | async-done | bytes 1048592 | tf_op jit(solution)/shard_map/all_gather | solution.py:78
  341.8 11.7 %cholesky.446 = f32[128,128]{1,0:T(8,128)S(1)} custom-call(f32[128,128]{1,0:T(8,128)S(1)} %cholesky.599), custom_call_target="Cholesky" | custom-call | tf_op jit(solution)/shard_map/jit(cholesky)/cholesky | solution.py:81
  364.2 11.7 %cholesky.465 = f32[128,128]{1,0:T(8,128)S(1)} custom-call(f32[128,128]{1,0:T(8,128)S(1)} %cholesky.603), custom_call_target="Cholesky" | custom-call | tf_op jit(solution)/shard_map/jit(cholesky)/cholesky | solution.py:81
  387.9 11.7 %cholesky.486 = f32[128,128]{1,0:T(8,128)S(1)} custom-call(f32[128,128]{1,0:T(8,128)S(1)} %cholesky.608), custom_call_target="Cholesky" | custom-call | tf_op jit(solution)/shard_map/jit(cholesky)/cholesky | solution.py:81
  410.7 11.7 %cholesky.503 = f32[128,128]{1,0:T(8,128)S(1)} custom-call(f32[128,128]{1,0:T(8,128)S(1)} %convolution_subtract_fusion.13), custom_call_target="Cholesky" | custom-call | tf_op jit(solution)/shard_map/jit(cholesky)/cholesky | solution.py:81
  437.4 39.9 %custom-call.42 = f32[4,128,128]{1,2,0:T(8,128)} custom-call(f32[4,128,128]{2,1,0:T(8,128)S(1)} %get-tuple-element.49), custom_call_target="InvertDiagBlocksLowerTriangular" | custom-call | tf_op jit(solution)/shard_map/triangular_solve/custom-call.3 | solution.py:16
  491.8 10.6 %while.15 = (s32[]{:T(128)}, f32[512,512]{1,0:T(8,128)S(1)}, s32[4,2]{0,1:T(2,128)S(1)}, f32[4,128,128]{2,1,0:T(8,128)}, s32[]{:T(128)}) while((s32[]{:T(128)}, f32[512,512]{1,0:T(8,128)S(1)}, s32[4,2]{0,1:T(2,128)S(1)}, f32[4,128,128]{2,1,0:T(8,128)}, s32[]{:T(128)}) %tuple.157), condition=%wide.while_cond.clone.2, body=%wide.while_body.clone.2.sunk | while | flops 2 | bytes 132705 | solution.py:16
  502.4 40.8 %custom-call.43 = f32[4,128,128]{1,2,0:T(8,128)} custom-call(f32[4,128,128]{2,1,0:T(8,128)} %get-tuple-element.50), custom_call_target="InvertDiagBlocksLowerTriangular" | custom-call | tf_op jit(solution)/shard_map/triangular_solve/custom-call.3 | solution.py:16
  558.6 22.8 %collective-permute-done.10 = f32[512,512]{1,0:T(8,128)S(1)} collective-permute-done((f32[512,512]{1,0:T(8,128)S(1)}, f32[512,512]{1,0:T(8,128)S(1)}, u32[]{:S(2)}, u32[]{:S(2)}) %collective-permute-start.10) | collective-permute-done | bytes 1048608 | tf_op jit(solution)/shard_map/ppermute | solution.py:12
  590.4 11.7 %cholesky.518 = f32[128,128]{1,0:T(8,128)S(1)} custom-call(f32[128,128]{1,0:T(8,128)S(1)} %cholesky.612), custom_call_target="Cholesky" | custom-call | tf_op jit(solution)/shard_map/jit(cholesky)/cholesky | solution.py:81
  612.8 11.7 %cholesky.537 = f32[128,128]{1,0:T(8,128)S(1)} custom-call(f32[128,128]{1,0:T(8,128)S(1)} %cholesky.616), custom_call_target="Cholesky" | custom-call | tf_op jit(solution)/shard_map/jit(cholesky)/cholesky | solution.py:81
  636.7 11.7 %cholesky.558 = f32[128,128]{1,0:T(8,128)S(1)} custom-call(f32[128,128]{1,0:T(8,128)S(1)} %cholesky.621), custom_call_target="Cholesky" | custom-call | tf_op jit(solution)/shard_map/jit(cholesky)/cholesky | solution.py:81
  659.6 11.9 %cholesky.575 = f32[128,128]{1,0:T(8,128)S(1)} custom-call(f32[128,128]{1,0:T(8,128)S(1)} %convolution_subtract_fusion.12), custom_call_target="Cholesky" | custom-call | tf_op jit(solution)/shard_map/jit(cholesky)/cholesky | solution.py:81
  687.1 39.9 %custom-call.47 = f32[4,128,128]{1,2,0:T(8,128)} custom-call(f32[4,128,128]{2,1,0:T(8,128)S(1)} %get-tuple-element.51), custom_call_target="InvertDiagBlocksLowerTriangular" | custom-call | tf_op jit(solution)/shard_map/triangular_solve/custom-call.3 | solution.py:16
  758.0 40.8 %custom-call.48 = f32[4,128,128]{1,2,0:T(8,128)} custom-call(f32[4,128,128]{2,1,0:T(8,128)} %get-tuple-element.52), custom_call_target="InvertDiagBlocksLowerTriangular" | custom-call | tf_op jit(solution)/shard_map/triangular_solve/custom-call.3 | solution.py:16
  (307 shorter events, 359.4 us)
Async XLA Ops:
  7.2 85.6 %all-gather.8.cloned.1.call-start = ((), (), s32[]{:S(2)}) async-start(), calls=%async_computation | async-start | bytes 1310720 | tf_op jit(solution)/shard_map/all_gather | solution.py:78
  13.9 7.7 collective-permute-start.1
  21.6 15.2 %collective-permute-start.2 = (bf16[512,512]{1,0:T(8,128)(2,1)S(1)}, bf16[512,512]{1,0:T(8,128)(2,1)S(1)}, u32[]{:S(2)}, u32[]{:S(2)}) collective-permute-start(bf16[512,512]{1,0:T(8,128)(2,1)S(1)} %bitcast.250), channel_id=1, source_target_pairs={{0,1},{1,2},{2,3},{3,0},{4,5},{5,6},{6,7},{7,4},{8,9},{9,10},{10,1... | collective-permute-start | bytes 1572872 | tf_op jit(solution)/shard_map/ppermute | solution.py:61
  36.9 14.3 %collective-permute-start.3 = (bf16[512,512]{1,0:T(8,128)(2,1)S(1)}, bf16[512,512]{1,0:T(8,128)(2,1)S(1)}, u32[]{:S(2)}, u32[]{:S(2)}) collective-permute-start(bf16[512,512]{1,0:T(8,128)(2,1)S(1)} %collective-permute-done.2), channel_id=1, source_target_pairs={{0,1},{1,2},{2,3},{3,0},{4,5},{5,6},{6,7},{7,4},{8,9},{9,10},{10,1... | collective-permute-start | bytes 1572872 | tf_op jit(solution)/shard_map/ppermute | solution.py:61
  39.0 13.3 %collective-permute-start.4 = (bf16[512,512]{1,0:T(8,128)(2,1)S(1)}, bf16[512,512]{1,0:T(8,128)(2,1)S(1)}, u32[]{:S(2)}, u32[]{:S(2)}) collective-permute-start(bf16[512,512]{1,0:T(8,128)(2,1)S(1)} %bitcast.251), channel_id=1, source_target_pairs={{0,3},{1,0},{2,1},{3,2},{4,7},{5,4},{6,5},{7,6},{8,11},{9,8},{10,9... | collective-permute-start | bytes 1572872 | tf_op jit(solution)/shard_map/ppermute | solution.py:63
  44.0 8.5 %collective-permute-start = (bf16[1,128,512]{1,2,0:T(8,128)(2,1)S(1)}, bf16[1,128,512]{1,2,0:T(8,128)(2,1)S(1)}, u32[]{:S(2)}, u32[]{:S(2)}) collective-permute-start(bf16[1,128,512]{1,2,0:T(8,128)(2,1)S(1)} %copy.20), channel_id=1, source_target_pairs={{0,4},{4,8},{8,12},{12,16},{16,20},{20,24},{24,28},{28,32},{32,36}... | collective-permute-start | bytes 393224 | tf_op jit(solution)/shard_map/ppermute | solution.py:12
  54.5 174.8 %all-gather.18.cloned.1.call-start = ((), (), s32[]{:S(2)}) async-start(), calls=%async_computation.5 | async-start | bytes 1310720 | tf_op jit(solution)/shard_map/all_gather | solution.py:79
  55.3 283.5 %all-gather.10.cloned.1.call-start = ((), (), s32[]{:S(2)}) async-start(), calls=%async_computation.1 | async-start | bytes 1310720 | tf_op jit(solution)/shard_map/all_gather | solution.py:78
  180.1 62.9 %collective-permute-start.6 = (f32[512,512]{1,0:T(8,128)S(1)}, f32[512,512]{1,0:T(8,128)}, u32[]{:S(2)}, u32[]{:S(2)}) collective-permute-start(f32[512,512]{1,0:T(8,128)S(1)} %get-tuple-element.110), channel_id=1, source_target_pairs={{4,0},{8,4},{12,8},{16,12},{20,16},{24,20},{28,24},{32,28},{36,32}... | collective-permute-start | bytes 3145736 | tf_op jit(solution)/shard_map/ppermute | solution.py:12
  235.0 61.2 %copy-start.2 = (f32[1,512,512]{1,2,0:T(8,128)S(1)}, f32[1,512,512]{1,2,0:T(8,128)}, u32[]{:S(2)}) copy-start(f32[1,512,512]{1,2,0:T(8,128)} %all-gather.18.cloned.1.call-done) | copy-start | bytes 3145732
  240.6 62.3 %collective-permute-start.5 = (f32[128,512]{0,1:T(8,128)}, f32[128,512]{0,1:T(8,128)}, u32[]{:S(2)}, u32[]{:S(2)}) collective-permute-start(f32[128,512]{0,1:T(8,128)} %fusion.104), channel_id=1, source_target_pairs={{0,4},{4,8},{8,12},{12,16},{16,20},{20,24},{24,28},{28,32},{32,36}... | collective-permute-start | bytes 786440 | tf_op jit(solution)/shard_map/ppermute | solution.py:12
  255.5 47.4 %copy-start.5 = (f32[128,512]{0,1:T(8,128)S(1)}, f32[128,512]{0,1:T(8,128)}, u32[]{:S(2)}) copy-start(f32[128,512]{0,1:T(8,128)} %fusion.72) | copy-start | bytes 786436
  306.4 171.0 %all-gather.12.cloned.1.call-start = ((), (), s32[]{:S(2)}) async-start(), calls=%async_computation.2 | async-start | bytes 1310720 | tf_op jit(solution)/shard_map/all_gather | solution.py:79
  306.4 15.5 %collective-permute-start.7 = (f32[512,512]{1,0:T(8,128)S(1)}, f32[512,512]{1,0:T(8,128)S(1)}, u32[]{:S(2)}, u32[]{:S(2)}) collective-permute-start(f32[512,512]{1,0:T(8,128)S(1)} %pad_maximum_fusion), channel_id=1, source_target_pairs={{4,0},{8,4},{12,8},{16,12},{20,16},{24,20},{28,24},{32,28},{36,32}... | collective-permute-start | bytes 3145736 | tf_op jit(solution)/shard_map/ppermute | solution.py:12
  323.4 264.0 %all-gather.14.cloned.1.call-start = ((), (), s32[]{:S(2)}) async-start(), calls=%async_computation.3 | async-start | bytes 1310720 | tf_op jit(solution)/shard_map/all_gather | solution.py:78
  426.2 63.5 %collective-permute-start.9 = (f32[512,512]{1,0:T(8,128)S(1)}, f32[512,512]{1,0:T(8,128)}, u32[]{:S(2)}, u32[]{:S(2)}) collective-permute-start(f32[512,512]{1,0:T(8,128)S(1)} %get-tuple-element.108), channel_id=1, source_target_pairs={{8,0},{12,4},{16,8},{20,12},{24,16},{28,20},{32,24},{36,28},{40,32... | collective-permute-start | bytes 3145736 | tf_op jit(solution)/shard_map/ppermute | solution.py:12
  487.0 64.5 %collective-permute-start.8 = (f32[128,512]{0,1:T(8,128)}, f32[128,512]{0,1:T(8,128)}, u32[]{:S(2)}, u32[]{:S(2)}) collective-permute-start(f32[128,512]{0,1:T(8,128)} %fusion.102), channel_id=1, source_target_pairs={{0,8},{4,12},{8,16},{12,20},{16,24},{20,28},{24,32},{28,36},{32,40... | collective-permute-start | bytes 786440 | tf_op jit(solution)/shard_map/ppermute | solution.py:12
  502.4 49.1 %copy-start.4 = (f32[128,512]{0,1:T(8,128)S(1)}, f32[128,512]{0,1:T(8,128)}, u32[]{:S(2)}) copy-start(f32[128,512]{0,1:T(8,128)} %subtract_subtract_fusion.1) | copy-start | bytes 786436
  555.0 172.0 %all-gather.16.cloned.1.call-start = ((), (), s32[]{:S(2)}) async-start(), calls=%async_computation.4 | async-start | bytes 1310720 | tf_op jit(solution)/shard_map/all_gather | solution.py:79
  555.0 26.3 %collective-permute-start.10 = (f32[512,512]{1,0:T(8,128)S(1)}, f32[512,512]{1,0:T(8,128)S(1)}, u32[]{:S(2)}, u32[]{:S(2)}) collective-permute-start(f32[512,512]{1,0:T(8,128)S(1)} %pad_maximum_fusion.2), channel_id=1, source_target_pairs={{8,0},{12,4},{16,8},{20,12},{24,16},{28,20},{32,24},{36,28},{40,32... | collective-permute-start | bytes 3145736 | tf_op jit(solution)/shard_map/ppermute | solution.py:12
  675.0 70.8 %collective-permute-start.12 = (f32[512,512]{1,0:T(8,128)S(1)}, f32[512,512]{1,0:T(8,128)}, u32[]{:S(2)}, u32[]{:S(2)}) collective-permute-start(f32[512,512]{1,0:T(8,128)S(1)} %get-tuple-element.106), channel_id=1, source_target_pairs={{16,0},{20,4},{24,8},{28,12},{32,16},{36,20},{40,24},{44,28},{48,3... | collective-permute-start | bytes 3145736 | tf_op jit(solution)/shard_map/ppermute | solution.py:12
  734.2 76.5 %collective-permute-start.13 = (f32[512,512]{1,0:T(8,128)S(1)}, f32[512,512]{1,0:T(8,128)}, u32[]{:S(2)}, u32[]{:S(2)}) collective-permute-start(f32[512,512]{1,0:T(8,128)S(1)} %pad_maximum_fusion.4), channel_id=1, source_target_pairs={{16,0},{20,4},{24,8},{28,12},{32,16},{36,20},{40,24},{44,28},{48,3... | collective-permute-start | bytes 3145736 | tf_op jit(solution)/shard_map/ppermute | solution.py:12
  739.1 67.9 %collective-permute-start.11 = (f32[128,512]{0,1:T(8,128)}, f32[128,512]{0,1:T(8,128)}, u32[]{:S(2)}, u32[]{:S(2)}) collective-permute-start(f32[128,512]{0,1:T(8,128)} %fusion.100), channel_id=1, source_target_pairs={{0,16},{4,20},{8,24},{12,28},{16,32},{20,36},{24,40},{28,44},{32,4... | collective-permute-start | bytes 786440 | tf_op jit(solution)/shard_map/ppermute | solution.py:12
  758.0 49.1 %copy-start.3 = (f32[128,512]{0,1:T(8,128)S(1)}, f32[128,512]{0,1:T(8,128)}, u32[]{:S(2)}) copy-start(f32[128,512]{0,1:T(8,128)} %subtract_subtract_fusion) | copy-start | bytes 786436
  (4 other events, 54.9 us)
Sparse Core Ops, SparseCore 0:
  54.6 38.1 all-gather.7
  95.4 31.9 all-gather.17
  306.5 32.2 all-gather.9
  341.3 30.7 all-gather.11
  555.1 32.2 all-gather.13
  589.9 30.7 all-gather.15
